TPU v7x, 32 devices: a whole 2x2x4 slice. The times are simulated.
32 devices in a mesh: dp: 8 (over z, x), tp: 4 (over y, core).
Axes of the slice: x: 2, y: 2, z: 4, core: 2. Of those that a mesh axis runs over, the one named last changes fastest.
Arguments:
- query_stream: bfloat16 [32, 1024, 512], P('dp', 'tp'), may hold values from -6 to 6
- token_embed: bfloat16 [32, 1024, 512], P('dp', 'tp'), may hold values from -6 to 6
- encoder_out: bfloat16 [32, 1024, 512], P('dp', 'tp'), may hold values from -6 to 6
- out_grad: bfloat16 [32, 1024, 512], P('dp', 'tp'), may hold values from -6 to 6
- attn_q: bfloat16 [512, 512], P('dp', 'tp'), may hold values from -0.25 to 0.25
- attn_k: bfloat16 [512, 512], P('dp', 'tp'), may hold values from -0.25 to 0.25
- attn_v: bfloat16 [512, 512], P('dp', 'tp'), may hold values from -0.25 to 0.25
- attn_o: bfloat16 [512, 512], P('tp', 'dp'), may hold values from -1 to 1
- cross_q: bfloat16 [512, 512], P('dp', 'tp'), may hold values from -0.25 to 0.25
- cross_k: bfloat16 [512, 512], P('dp', 'tp'), may hold values from -0.25 to 0.25
- cross_v: bfloat16 [512, 512], P('dp', 'tp'), may hold values from -0.25 to 0.25
- cross_o: bfloat16 [512, 512], P('tp', 'dp'), may hold values from -1 to 1
- ffn_in: bfloat16 [512, 2048], P('dp', 'tp'), may hold values from -0.25 to 0.25
- ffn_bias_in: bfloat16 [2048], P(('tp', 'dp')), may hold values from -3 to 3
- ffn_out: bfloat16 [2048, 512], P('tp', 'dp'), may hold values from -0.125 to 0.125
- ffn_bias_out: float32 [512], replicated, may hold values from -3 to 3
- norm_gain: float32 [3, 512], replicated, may hold values from 0.1 to 1.9
- norm_bias: float32 [3, 512], replicated, may hold values from -2 to 2
- doc_lengths: int32 [32, 8], P('dp'), may hold values from 1 to 1017, as said below
- src_lengths: int32 [32, 8], P('dp'), may hold values from 1 to 1017, as said below
- ctx_rank: int32 [32, 1024], P('dp'), may hold values from 0 to 1023
- ctx_limit: int32 [32, 1024], P('dp'), may hold values from 1 to 1024
Outputs:
- mixed: bfloat16 [32, 1024, 512], P('dp', 'tp')
- grad_query: float32 [32, 1024, 512], P('dp', 'tp')
- grad_embed: float32 [32, 1024, 512], P('dp', 'tp')
- grad_encoder: float32 [32, 1024, 512], P('dp', 'tp')
- grad_attn_q: float32 [512, 512], P('dp', 'tp')
- grad_attn_k: float32 [512, 512], P('dp', 'tp')
- grad_attn_v: float32 [512, 512], P('dp', 'tp')
- grad_attn_o: float32 [512, 512], P('tp', 'dp')
- grad_cross_q: float32 [512, 512], P('dp', 'tp')
- grad_cross_k: float32 [512, 512], P('dp', 'tp')
- grad_cross_v: float32 [512, 512], P('dp', 'tp')
- grad_cross_o: float32 [512, 512], P('tp', 'dp')
- grad_ffn_in: float32 [512, 2048], P('dp', 'tp')
- grad_ffn_bias_in: float32 [2048], P(('tp', 'dp'))
- grad_ffn_out: float32 [2048, 512], P('tp', 'dp')
- grad_ffn_bias_out: float32 [512], replicated
- grad_norm_gain: float32 [3, 512], replicated
- grad_norm_bias: float32 [3, 512], replicated
Inputs may be any that keep to these rules, and one draw needn't show every extreme that they name: `doc_lengths`: in every row the 8 lengths sum to 1024; one of them, at a slot drawn from the seed, is a document that takes the rest of the row, the others are sentences of at most 32 tokens; in one row drawn from the seed all those sentences have one token. `src_lengths`: in every row the 8 lengths sum to 1024; one of them, at a slot drawn from the seed, is a source document that takes the rest of the row, the others are sentences of at most 32 tokens; in one row drawn from the seed all those sentences have one token.
All inputs are finite; a program needn't handle non-finite values.
Results may differ from a plain program's by a relative error of at most 0.025.
Values may be sent and summed in bfloat16 or wider, within the bound.
A program may use at most 192 MiB of HBM per device.

v0:
```python
from types import SimpleNamespace

import jax
import jax.numpy as jnp
from jax import lax
from jax.experimental import pallas as pl
from jax.experimental.pallas import tpu as pltpu
from jax.sharding import PartitionSpec as P

HEADS = 8
LOW = jnp.bfloat16
WIDE = jnp.float32


EPSILON = 1e-05
score_tile = 512


def layer_norm(values, scale_vec, shift_vec):
    average = jnp.mean(values, axis=-1, keepdims=True)
    centred = values - average
    spread = jnp.mean(centred * centred, axis=-1, keepdims=True)
    return centred * lax.rsqrt(spread + EPSILON) * scale_vec + shift_vec


def gelu_exact(values):
    return 0.5 * values * (1.0 + lax.erf(values * 0.7071067811865476))


def project(inputs, matrix):
    return jnp.einsum("rld,de->rle", inputs, matrix, preferred_element_type=jnp.float32)


def project_back(cotangent, matrix):
    return jnp.einsum("rle,de->rld", cotangent, matrix, preferred_element_type=jnp.float32)


def outer_sum(inputs, cotangent):
    return jnp.einsum("rld,rle->de", inputs, cotangent, preferred_element_type=jnp.float32)


def layout(lengths, length):
    offsets = jnp.cumsum(lengths) - lengths
    positions = jnp.arange(length, dtype=jnp.int32)
    passed = positions[:, None] >= offsets[None, :]
    document = jnp.sum(passed.astype(jnp.int32), axis=1) - 1
    doc_start = jnp.max(jnp.where(passed, offsets[None, :], 0), axis=1)
    return (document, doc_start)


def self_visible(lengths, rank_row, limit_row, length, first_row, block_rows):
    document, doc_start = layout(lengths, length)
    positions = jnp.arange(length, dtype=jnp.int32)
    rows_pos = positions[first_row : first_row + block_rows]
    same_text = document[first_row : first_row + block_rows, None] == document[None, :]
    chosen = (rank_row[None, :] < limit_row[first_row : first_row + block_rows, None]) & (
        rows_pos[:, None] != positions[None, :]
    )
    opener = positions[None, :] == doc_start[first_row : first_row + block_rows, None]
    return same_text & (chosen | opener)


def cross_visible(lengths, src_lengths, length, src_length, first_row, block_rows):
    document, _ = layout(lengths, length)
    source_doc, _ = layout(src_lengths, src_length)
    return document[first_row : first_row + block_rows, None] == source_doc[None, :]


def attend_forward(queries, keys_all, values_all, visible_of, head_count):
    query_count = queries.shape[0]
    head_size = queries.shape[1] // head_count
    factor = head_size ** (-0.5)
    queries = queries.reshape(query_count, head_count, head_size)
    keys_all = keys_all.reshape(keys_all.shape[0], head_count, head_size)
    values_all = values_all.reshape(values_all.shape[0], head_count, head_size)
    block_rows = min(score_tile, query_count)
    outputs = []
    totals = []
    for first_row in range(0, query_count, block_rows):
        query_part = queries[first_row : first_row + block_rows]
        scores = (
            jnp.einsum("qhd,khd->hqk", query_part, keys_all, preferred_element_type=jnp.float32)
            * factor
        )
        scores = jnp.where(visible_of(first_row, block_rows)[None], scores, -1e30)
        highest = jnp.max(scores, axis=-1, keepdims=True)
        exponent = jnp.exp(scores - highest)
        denominator = jnp.sum(exponent, axis=-1, keepdims=True)
        weights_low = (exponent / denominator).astype(jnp.bfloat16)
        outputs.append(
            jnp.einsum("hqk,khd->qhd", weights_low, values_all, preferred_element_type=jnp.float32)
        )
        totals.append(highest[..., 0] + jnp.log(denominator[..., 0]))
    context = jnp.concatenate(outputs, axis=0).reshape(query_count, head_count * head_size)
    return (context, jnp.concatenate(totals, axis=1))


def attend_backward(queries, keys_all, values_all, visible_of, totals, grad_context, head_count):
    query_count = queries.shape[0]
    key_count = keys_all.shape[0]
    head_size = queries.shape[1] // head_count
    factor = head_size ** (-0.5)
    queries = queries.reshape(query_count, head_count, head_size)
    keys_all = keys_all.reshape(key_count, head_count, head_size)
    values_all = values_all.reshape(key_count, head_count, head_size)
    grad_context = grad_context.reshape(query_count, head_count, head_size)
    grad_keys = jnp.zeros((key_count, head_count, head_size), jnp.float32)
    grad_values = jnp.zeros((key_count, head_count, head_size), jnp.float32)
    grad_queries = []
    block_rows = min(score_tile, query_count)
    for first_row in range(0, query_count, block_rows):
        query_part = queries[first_row : first_row + block_rows]
        grad_part = grad_context[first_row : first_row + block_rows]
        scores = (
            jnp.einsum("qhd,khd->hqk", query_part, keys_all, preferred_element_type=jnp.float32)
            * factor
        )
        scores = jnp.where(visible_of(first_row, block_rows)[None], scores, -1e30)
        weights_full = jnp.exp(scores - totals[:, first_row : first_row + block_rows, None])
        grad_weights = jnp.einsum(
            "qhd,khd->hqk", grad_part, values_all, preferred_element_type=jnp.float32
        )
        inner = jnp.sum(grad_weights * weights_full, axis=-1, keepdims=True)
        grad_scores = (weights_full * (grad_weights - inner)).astype(jnp.bfloat16)
        grad_queries.append(
            jnp.einsum("hqk,khd->qhd", grad_scores, keys_all, preferred_element_type=jnp.float32)
            * factor
        )
        grad_keys = (
            grad_keys
            + jnp.einsum(
                "hqk,qhd->khd", grad_scores, query_part, preferred_element_type=jnp.float32
            )
            * factor
        )
        grad_values = grad_values + jnp.einsum(
            "hqk,qhd->khd",
            weights_full.astype(jnp.bfloat16),
            grad_part,
            preferred_element_type=jnp.float32,
        )
    grad_queries = jnp.concatenate(grad_queries, axis=0).reshape(
        query_count, head_count * head_size
    )
    return (
        grad_queries.astype(jnp.bfloat16),
        grad_keys.reshape(key_count, -1).astype(jnp.bfloat16),
        grad_values.reshape(key_count, -1).astype(jnp.bfloat16),
    )


def collect(piece):
    return lax.all_gather(piece, "tp", axis=1, tiled=True)


def spread_sum(partial_sum):
    return lax.psum_scatter(partial_sum, "tp", scatter_dimension=1, tiled=True)


def collect_grad(piece):
    return lax.all_gather(piece, "tp", axis=1, tiled=True)


def send_back(partial_sum):
    return lax.psum_scatter(partial_sum, "tp", scatter_dimension=1, tiled=True)


def local_split(
    query_stream,
    token_embed,
    encoder_out,
    out_grad,
    attn_q,
    attn_k,
    attn_v,
    attn_o,
    cross_q,
    cross_k,
    cross_v,
    cross_o,
    ffn_in,
    ffn_bias_in,
    ffn_out,
    ffn_bias_out,
    norm_gain,
    norm_bias,
    doc_lengths,
    src_lengths,
    ctx_rank,
    ctx_limit,
):
    head_count = HEADS // lax.axis_size("tp")
    (
        self_query,
        self_key,
        self_value,
        self_out,
        other_query,
        other_key,
        other_value,
        other_out,
        hidden_in,
        hidden_bias,
        hidden_out,
    ) = (
        lax.all_gather(attn_q, "dp", axis=0, tiled=True),
        lax.all_gather(attn_k, "dp", axis=0, tiled=True),
        lax.all_gather(attn_v, "dp", axis=0, tiled=True),
        lax.all_gather(attn_o, "dp", axis=1, tiled=True),
        lax.all_gather(cross_q, "dp", axis=0, tiled=True),
        lax.all_gather(cross_k, "dp", axis=0, tiled=True),
        lax.all_gather(cross_v, "dp", axis=0, tiled=True),
        lax.all_gather(cross_o, "dp", axis=1, tiled=True),
        lax.all_gather(ffn_in, "dp", axis=0, tiled=True),
        lax.all_gather(ffn_bias_in, "dp", axis=0, tiled=True),
        lax.all_gather(ffn_out, "dp", axis=1, tiled=True),
    )

    def self_forward(row_items):
        queries, keys_all, values_all, lengths, rank_row, limit_row = row_items

        def visible_of(first_row, block_rows):
            return self_visible(
                lengths, rank_row, limit_row, keys_all.shape[0], first_row, block_rows
            )

        return attend_forward(queries, keys_all, values_all, visible_of, head_count)

    def self_backward(row_items):
        queries, keys_all, values_all, lengths, rank_row, limit_row, totals, grad_context = (
            row_items
        )

        def visible_of(first_row, block_rows):
            return self_visible(
                lengths, rank_row, limit_row, keys_all.shape[0], first_row, block_rows
            )

        return attend_backward(
            queries, keys_all, values_all, visible_of, totals, grad_context, head_count
        )

    def cross_forward(row_items):
        queries, keys_all, values_all, lengths, source_lengths = row_items

        def visible_of(first_row, block_rows):
            return cross_visible(
                lengths, source_lengths, queries.shape[0], keys_all.shape[0], first_row, block_rows
            )

        return attend_forward(queries, keys_all, values_all, visible_of, head_count)

    def cross_backward(row_items):
        queries, keys_all, values_all, lengths, source_lengths, totals, grad_context = row_items

        def visible_of(first_row, block_rows):
            return cross_visible(
                lengths, source_lengths, queries.shape[0], keys_all.shape[0], first_row, block_rows
            )

        return attend_backward(
            queries, keys_all, values_all, visible_of, totals, grad_context, head_count
        )

    query_all = collect(query_stream)
    embed_all = collect(token_embed)
    source_all = collect(encoder_out)
    self_queries = project(query_all, self_query).astype(jnp.bfloat16)
    self_keys = project(embed_all, self_key).astype(jnp.bfloat16)
    self_values = project(embed_all, self_value).astype(jnp.bfloat16)
    self_context, self_totals = lax.map(
        self_forward, (self_queries, self_keys, self_values, doc_lengths, ctx_rank, ctx_limit)
    )
    self_low = self_context.astype(jnp.bfloat16)
    first_sum = query_stream.astype(jnp.float32) + spread_sum(project(self_low, self_out))
    hidden_one, first_back = jax.vjp(layer_norm, first_sum, norm_gain[0], norm_bias[0])
    hidden_one_all = collect(hidden_one.astype(jnp.bfloat16))
    cross_queries = project(hidden_one_all, other_query).astype(jnp.bfloat16)
    cross_keys = project(source_all, other_key).astype(jnp.bfloat16)
    cross_values = project(source_all, other_value).astype(jnp.bfloat16)
    cross_context, cross_totals = lax.map(
        cross_forward, (cross_queries, cross_keys, cross_values, doc_lengths, src_lengths)
    )
    cross_low = cross_context.astype(jnp.bfloat16)
    second_sum = hidden_one + spread_sum(project(cross_low, other_out))
    hidden_two, second_back = jax.vjp(layer_norm, second_sum, norm_gain[1], norm_bias[1])
    hidden_two_low = hidden_two.astype(jnp.bfloat16)
    ffn_inputs = lax.all_gather(hidden_two_low, "tp", axis=1, tiled=True)
    ffn_pre = project(ffn_inputs, hidden_in) + hidden_bias.astype(jnp.float32)
    ffn_gate, gelu_back = jax.vjp(gelu_exact, ffn_pre)
    ffn_act = ffn_gate.astype(jnp.bfloat16)
    ffn_branch = (
        lax.psum_scatter(project(ffn_act, hidden_out), "tp", scatter_dimension=1, tiled=True)
        + ffn_bias_out
    )
    third_sum = hidden_two + ffn_branch
    mixed_full, third_back = jax.vjp(layer_norm, third_sum, norm_gain[2], norm_bias[2])
    grad_third, gain_two, shift_two = third_back(out_grad.astype(jnp.float32))
    grad_ffn = grad_third.astype(jnp.bfloat16)
    grad_bias_out = jnp.sum(grad_ffn.astype(jnp.float32), axis=(0, 1))
    grad_ffn_all = lax.all_gather(grad_ffn, "tp", axis=1, tiled=True)
    grad_act = project_back(grad_ffn_all, hidden_out)
    grad_down = outer_sum(ffn_act, grad_ffn_all)
    grad_pre = gelu_back(grad_act)[0].astype(jnp.bfloat16)
    grad_up = outer_sum(ffn_inputs, grad_pre)
    grad_bias_in = jnp.sum(grad_pre.astype(jnp.float32), axis=(0, 1))
    grad_two = grad_third + lax.psum_scatter(
        project_back(grad_pre, hidden_in), "tp", scatter_dimension=1, tiled=True
    )
    grad_second, gain_one, shift_one = second_back(grad_two)
    grad_cross_all = collect_grad(grad_second.astype(jnp.bfloat16))
    grad_other_out = outer_sum(cross_low, grad_cross_all)
    grad_cross_ctx = project_back(grad_cross_all, other_out).astype(jnp.bfloat16)
    cross_dq, cross_dk, cross_dv = lax.map(
        cross_backward,
        (
            cross_queries,
            cross_keys,
            cross_values,
            doc_lengths,
            src_lengths,
            cross_totals,
            grad_cross_ctx,
        ),
    )
    grad_other_query = outer_sum(hidden_one_all, cross_dq)
    grad_other_key = outer_sum(source_all, cross_dk)
    grad_other_value = outer_sum(source_all, cross_dv)
    grad_encoder = send_back(
        project_back(cross_dk, other_key) + project_back(cross_dv, other_value)
    )
    grad_one = grad_second + send_back(project_back(cross_dq, other_query))
    grad_first, gain_zero, shift_zero = first_back(grad_one)
    grad_attn_all = collect_grad(grad_first.astype(jnp.bfloat16))
    grad_self_out = outer_sum(self_low, grad_attn_all)
    grad_self_ctx = project_back(grad_attn_all, self_out).astype(jnp.bfloat16)
    self_dq, self_dk, self_dv = lax.map(
        self_backward,
        (
            self_queries,
            self_keys,
            self_values,
            doc_lengths,
            ctx_rank,
            ctx_limit,
            self_totals,
            grad_self_ctx,
        ),
    )
    grad_self_query = outer_sum(query_all, self_dq)
    grad_self_key = outer_sum(embed_all, self_dk)
    grad_self_value = outer_sum(embed_all, self_dv)
    grad_embed = send_back(project_back(self_dk, self_key) + project_back(self_dv, self_value))
    grad_query = grad_first + send_back(project_back(self_dq, self_query))
    (
        grad_self_query,
        grad_self_key,
        grad_self_value,
        grad_self_out,
        grad_other_query,
        grad_other_key,
        grad_other_value,
        grad_other_out,
        grad_up,
        grad_bias_in,
        grad_down,
    ) = (
        lax.psum_scatter(
            grad_self_query.astype(jnp.bfloat16), "dp", scatter_dimension=0, tiled=True
        ).astype(jnp.float32),
        lax.psum_scatter(
            grad_self_key.astype(jnp.bfloat16), "dp", scatter_dimension=0, tiled=True
        ).astype(jnp.float32),
        lax.psum_scatter(
            grad_self_value.astype(jnp.bfloat16), "dp", scatter_dimension=0, tiled=True
        ).astype(jnp.float32),
        lax.psum_scatter(
            grad_self_out.astype(jnp.bfloat16), "dp", scatter_dimension=1, tiled=True
        ).astype(jnp.float32),
        lax.psum_scatter(
            grad_other_query.astype(jnp.bfloat16), "dp", scatter_dimension=0, tiled=True
        ).astype(jnp.float32),
        lax.psum_scatter(
            grad_other_key.astype(jnp.bfloat16), "dp", scatter_dimension=0, tiled=True
        ).astype(jnp.float32),
        lax.psum_scatter(
            grad_other_value.astype(jnp.bfloat16), "dp", scatter_dimension=0, tiled=True
        ).astype(jnp.float32),
        lax.psum_scatter(
            grad_other_out.astype(jnp.bfloat16), "dp", scatter_dimension=1, tiled=True
        ).astype(jnp.float32),
        lax.psum_scatter(
            grad_up.astype(jnp.bfloat16), "dp", scatter_dimension=0, tiled=True
        ).astype(jnp.float32),
        lax.psum_scatter(
            grad_bias_in.astype(jnp.bfloat16), "dp", scatter_dimension=0, tiled=True
        ).astype(jnp.float32),
        lax.psum_scatter(
            grad_down.astype(jnp.bfloat16), "dp", scatter_dimension=1, tiled=True
        ).astype(jnp.float32),
    )
    gain_grads = jnp.stack([gain_zero, gain_one, gain_two])
    shift_grads = jnp.stack([shift_zero, shift_one, shift_two])
    gain_grads, shift_grads, grad_bias_out = lax.psum(
        (gain_grads, shift_grads, grad_bias_out), ("dp", "tp")
    )
    return (
        mixed_full.astype(jnp.bfloat16),
        grad_query,
        grad_embed,
        grad_encoder,
        grad_self_query,
        grad_self_key,
        grad_self_value,
        grad_self_out,
        grad_other_query,
        grad_other_key,
        grad_other_value,
        grad_other_out,
        grad_up,
        grad_bias_in,
        grad_down,
        grad_bias_out,
        gain_grads,
        shift_grads,
    )


HIDDEN = -1e30
Q_TILE = 256


def product(left, right, left_axis, right_axis):
    return lax.dot_general(
        left, right, (((left_axis,), (right_axis,)), ((), ())), preferred_element_type=WIDE
    )


def nn(left, right):
    return product(left, right, 1, 0)


def nt(left, right):
    return product(left, right, 1, 1)


def tn(left, right):
    return product(left, right, 0, 0)


def rows_of(index, size):
    return pl.ds(pl.multiple_of(index * size, size), size)


def normalize(values):
    average = jnp.mean(values, axis=-1, keepdims=True)
    centred = values - average
    spread = jnp.mean(centred * centred, axis=-1, keepdims=True)
    inverse = lax.rsqrt(spread + EPSILON)
    return centred * inverse, inverse


def normalize_back(grad, normal, inverse, gain):
    scaled = grad * gain
    mean_one = jnp.mean(scaled, axis=-1, keepdims=True)
    mean_two = jnp.mean(scaled * normal, axis=-1, keepdims=True)
    return inverse * (scaled - mean_one - normal * mean_two)


def add_rows(target, grad):
    target[...] += jnp.sum(grad, axis=0, keepdims=True)


def documents(lengths, row, shape, axis):
    positions = lax.broadcasted_iota(jnp.int32, shape, axis)
    document = jnp.full(shape, -1, jnp.int32)
    start = jnp.zeros(shape, jnp.int32)
    offset = jnp.int32(0)
    for slot in range(lengths.shape[1]):
        passed = positions >= offset
        document = document + passed.astype(jnp.int32)
        start = jnp.where(passed, offset, start)
        offset = offset + lengths[row, slot]
    return positions, document, start


def fill_self_bias(bias, lengths, rank, limit, row):
    length = bias.shape[0]
    key_position, key_document, _ = documents(lengths, row, (length, 1), 0)
    position, document, start = documents(lengths, row, (1, length), 1)
    rank_row = rank[pl.ds(row, 1), :].astype(WIDE)
    key_rank = jnp.transpose(jnp.broadcast_to(rank_row, (128, length)))[:, :1]
    query_limit = limit[pl.ds(row, 1), :].astype(WIDE)
    for tile in range(length // Q_TILE):
        part = slice(tile * Q_TILE, (tile + 1) * Q_TILE)
        chosen = (key_rank < query_limit[:, part]) & (key_position != position[:, part])
        seen = (key_document == document[:, part]) & (chosen | (key_position == start[:, part]))
        bias[:, part] = jnp.where(seen, 0.0, HIDDEN).astype(bias.dtype)


def fill_cross_bias(bias, lengths, source_lengths, row):
    length = bias.shape[0]
    _, key_document, _ = documents(source_lengths, row, (length, 1), 0)
    _, document, _ = documents(lengths, row, (1, length), 1)
    for tile in range(length // Q_TILE):
        part = slice(tile * Q_TILE, (tile + 1) * Q_TILE)
        seen = key_document == document[:, part]
        bias[:, part] = jnp.where(seen, 0.0, HIDDEN).astype(bias.dtype)


def one_head(pair, side):
    lane = lax.broadcasted_iota(jnp.int32, pair.shape, 1)
    return jnp.where(lane // 64 == side, pair, jnp.zeros_like(pair))


def run_after(step, after):
    for number, actions in after.items():
        if actions:

            @pl.when(step == number)
            def _():
                for action in actions:
                    action()


PAIRS = HEADS // 2


class Kept:
    def __init__(self, kept, room, sems, place_of=lambda step: step):
        self.kept, self.room, self.sems, self.place_of = kept, room, sems, place_of

    def slot(self, step, side=None):
        place = lax.rem(step, 4)
        if side is None:
            return rows_of(place, 2 * Q_TILE)
        return rows_of(2 * place + side, Q_TILE)

    def store(self, step):
        room = self.room.at[:, self.slot(step)]
        return pltpu.make_async_copy(room, self.kept.at[self.place_of(step)], self.sems.at[lax.rem(step, 4)])

    def load(self, step):
        room = self.room.at[:, self.slot(step)]
        return pltpu.make_async_copy(self.kept.at[self.place_of(step)], room, self.sems.at[lax.rem(step, 4)])


def attend(keys, queries, values_t, bias, context, inverses, tile_of, room, kept, after):
    scores_of, highest_of = room
    steps = keys.shape[0] // Q_TILE * PAIRS

    def where(step):
        return rows_of(tile_of(step // PAIRS), Q_TILE), lax.rem(step, PAIRS)

    def score(step, slot):
        part, pair = where(step)
        lanes = rows_of(pair, 128)
        for side in (0, 1):
            scores = nt(keys[:, lanes], one_head(queries[part, lanes], side))
            scores = scores + bias[:, part].astype(WIDE)
            scores_of[slot][:, side * Q_TILE : (side + 1) * Q_TILE] = scores
            highest_of[2 * slot + side] = jnp.max(scores, axis=0, keepdims=True)

    def weigh(step, slot):
        part, pair = where(step)
        outs = []
        for side in (0, 1):
            head = 2 * pair + side
            scores = scores_of[slot][:, side * Q_TILE : (side + 1) * Q_TILE]
            weights = jnp.exp(scores - highest_of[2 * slot + side]).astype(LOW)
            kept.room[:, kept.slot(step, side)] = weights
            out = nn(values_t[head], weights)
            inverse = 1.0 / out[64:65]
            outs.append(out[:64] * inverse)
            inverses[pl.ds(head, 1), part] = inverse
        context[part, rows_of(pair, 128)] = jnp.transpose(jnp.concatenate(outs, axis=0)).astype(LOW)

    score(0, 0)

    @pl.loop(0, steps // 2)
    def _(double):
        @pl.when(double > 1)
        def _():
            kept.store(2 * double - 4).wait()
            kept.store(2 * double - 3).wait()

        score(2 * double + 1, 1)
        weigh(2 * double, 0)
        score(lax.rem(2 * double + 2, steps), 0)
        weigh(2 * double + 1, 1)
        kept.store(2 * double).start()
        kept.store(2 * double + 1).start()
        run_after(double, after)

    for step in range(steps - 4, steps):
        kept.store(step).wait()


def attend_back(keys_t, queries, values, cotangent, inner, grads, tile_of, room, kept, after):
    key_sum, value_sum, grad_queries = grads
    steps = values.shape[0] // Q_TILE * PAIRS

    def where(step):
        return rows_of(tile_of(step // PAIRS), Q_TILE), rows_of(lax.rem(step, PAIRS), 128)

    def make(step, slot):
        part, lanes = where(step)
        pair = lax.rem(step, PAIRS)
        for side in (0, 1):
            head = 2 * pair + side
            grad_weights = nt(values[:, lanes], one_head(cotangent[part, lanes], side))
            weights = kept.room[:, kept.slot(step, side)].astype(WIDE)
            grad_scores = weights * (grad_weights - inner[pl.ds(head, 1), part])
            room[slot][:, side * Q_TILE : (side + 1) * Q_TILE] = grad_scores.astype(LOW)

    def use(step, slot):
        part, lanes = where(step)
        pair = lax.rem(step, PAIRS)

        def stacked(ref):
            return jnp.concatenate([one_head(ref[part, lanes], side) for side in (0, 1)], axis=0)

        outs = [
            nn(keys_t[2 * pair + side, :64], room[slot][:, side * Q_TILE : (side + 1) * Q_TILE])
            for side in (0, 1)
        ]
        turned = jnp.transpose(jnp.concatenate(outs, axis=0) * 0.125)
        grad_queries[part, lanes] = turned.astype(LOW)
        value_sum[:, lanes] += nn(kept.room[:, kept.slot(step)], stacked(cotangent))
        key_sum[:, lanes] += nn(room[slot][...], stacked(queries))

    key_sum[...] = jnp.zeros_like(key_sum)
    value_sum[...] = jnp.zeros_like(value_sum)
    kept.load(0).wait()
    make(0, 0)

    @pl.loop(0, steps // 2)
    def _(double):
        kept.load(2 * double + 1).wait()
        make(2 * double + 1, 1)
        use(2 * double, 0)

        @pl.when(double < steps // 2 - 1)
        def _():
            kept.load(2 * double + 2).wait()

        make(lax.rem(2 * double + 2, steps), 0)
        use(2 * double + 1, 1)

        @pl.when(double < steps // 2 - 2)
        def _():
            kept.load(2 * double + 4).start()
            kept.load(2 * double + 5).start()

        run_after(double, after)


def inner_products(cotangent, context, inner):
    products = cotangent[...].astype(WIDE) * context[...].astype(WIDE)
    high = products.astype(LOW)
    rest = (products - high.astype(WIDE)).astype(LOW)
    shape = (2 * HEADS, products.shape[1])
    head = lax.broadcasted_iota(jnp.int32, shape, 0)
    lane = lax.broadcasted_iota(jnp.int32, shape, 1)
    pick = jnp.where(lane // 64 == head, 1.0, 0.0).astype(LOW)
    inner[...] = (nt(pick, high) + nt(pick, rest))[:HEADS]


def flip_heads(values, flipped):
    turned = jnp.transpose(values[...])
    for head in range(HEADS):
        flipped[head, :64] = turned[64 * head : 64 * head + 64]

MESH = pl.DeviceIdType.MESH


class Place:
    def __init__(self):
        dp, tp = lax.axis_index("dp"), lax.axis_index("tp")
        self.dp, self.tp = dp, tp
        self.z, self.x = dp // 2, lax.rem(dp, 2)
        self.y, self.core = tp // 2, lax.rem(tp, 2)
        self.core_peer = (dp, 2 * self.y + 1 - self.core)
        self.y_peer = (dp, 2 * (1 - self.y) + self.core)
        self.far_peer = (dp, 2 * (1 - self.y) + 1 - self.core)
        self.x_peer = (2 * self.z + 1 - self.x, tp)
        self.z_steps = [lax.rem(self.z + step, 4) for step in range(4)]
        self.z_peers = [(2 * z + self.x, tp) for z in self.z_steps[1:]]
        self.summing = [self.core_peer, self.x_peer, self.y_peer] + self.z_peers

    def greet(self):
        for peer in self.summing + [self.far_peer]:
            barrier = pltpu.get_barrier_semaphore()
            pl.semaphore_signal(barrier, inc=1, device_id=peer, device_id_type=MESH)

    def meet(self):
        pl.semaphore_wait(pltpu.get_barrier_semaphore(), len(self.summing) + 1)

    def tile(self, number):
        side = lax.rem(self.y + 1 - number // 2, 2)
        return 2 * side + lax.rem(self.core + (number + 1) // 2, 2)

    def columns(self, width):
        return [
            pl.ds(pl.multiple_of(tp * width, width), width)
            for tp in (self.tp, self.y_peer[1], self.core_peer[1], self.far_peer[1])
        ]


class Exchange:
    def __init__(self, sends, recvs, number):
        self.sends, self.recvs, self.number = sends, recvs, number
        self.made = []
        self.arriving = []

    def send(self, source, target, peer):
        slot = len(self.made)

        def copy():
            return pltpu.make_async_remote_copy(
                src_ref=source(),
                dst_ref=target(),
                send_sem=self.sends.at[self.number, slot],
                recv_sem=self.recvs.at[self.number, slot],
                device_id=peer,
                device_id_type=MESH,
            )

        copy().start()
        self.made.append(copy)
        self.arriving.append(copy)

    def move(self, block, peer):
        self.send(block, block, peer)

    def arrive(self):
        for copy in self.arriving:
            copy().wait_recv()
        self.arriving = []

    def finish(self):
        for copy in self.made:
            copy().wait_send()


class Gather(Exchange):
    slots = 11

    def __init__(
        self, place, local, full, first, count, side, sides, sends, recvs, own_sems, number
    ):
        super().__init__(sends, recvs, number)
        self.place, self.full, self.items = place, full, pl.ds(first, count)
        width = local.shape[-1] // sides
        self.sides = [
            pl.ds(pl.multiple_of((tp * sides + side) * width, width), width)
            for tp in (place.tp, place.y_peer[1])
        ]
        p = place
        self.source = lambda: local.at[self.items, :, side * width : (side + 1) * width]
        self.target = lambda: full.at[self.items, p.z, p.x, :, self.sides[0]]
        self.own = lambda: pltpu.make_async_copy(
            self.source(), self.target(), own_sems.at[number]
        )

    def stage(self, number):
        p, full, items = self.place, self.full, self.items
        self.arrive()
        if number == 0:
            self.own().start()
            self.send(self.source, self.target, p.y_peer)
        elif number == 1:
            self.own().wait()
            for side in self.sides:
                for peer in p.z_peers:
                    self.move(lambda side=side: full.at[items, p.z, p.x, :, side], peer)
        elif number == 2:
            for side in self.sides:
                self.move(lambda side=side: full.at[items, :, p.x, :, side], p.x_peer)
        elif number == 3:
            for side in self.sides:
                self.move(lambda side=side: full.at[items, :, :, :, side], p.core_peer)


class ToRow(Exchange):
    slots = 3

    def __init__(self, place, local, row, sends, recvs, own_sems, number):
        super().__init__(sends, recvs, number)
        size = local.shape[1]
        p = place
        span = pl.ds(pl.multiple_of(p.tp * size, size), size)

        def here():
            return row.at[span]

        self.local, self.here = local, here
        self.peers = (p.y_peer, p.far_peer, p.core_peer)
        self.own = lambda: pltpu.make_async_copy(local.at[p.tp], here(), own_sems.at[number])

    def start(self):
        for peer in self.peers:
            self.send(lambda peer=peer: self.local.at[peer[1]], self.here, peer)
        self.own().start()

    def near(self):
        self.own().wait()
        self.arriving.pop()().wait_recv()

    def far(self):
        self.arrive()


class FromRow(Exchange):
    slots = 3

    def __init__(self, place, row, blocks, sends, recvs, own_sems, number):
        super().__init__(sends, recvs, number)
        size = blocks.shape[1]
        p = place
        self.peers = (p.y_peer, p.far_peer, p.core_peer)
        self.target = lambda: blocks.at[p.tp]

        def part(tp):
            return row.at[pl.ds(pl.multiple_of(tp * size, size), size)]

        self.part = part
        self.own = lambda: pltpu.make_async_copy(
            self.part(p.tp), self.target(), own_sems.at[number]
        )

    def give(self, number):
        if number == 3:
            self.own().start()
        else:
            peer = self.peers[number]
            self.send(lambda: self.part(peer[1]), self.target, peer)

    def give_all(self):
        for number in range(4):
            self.give(number)

    def wait(self):
        self.own().wait()
        self.arrive()


class Scatter(Exchange):
    slots = 8

    def __init__(
        self, place, parts, work, last, out, first, count, ready, sends, recvs, number
    ):
        super().__init__(sends, recvs, number)
        self.place, self.parts, self.work, self.last, self.out = place, parts, work, last, out
        self.numbers = range(first, first + count)
        self.items = pl.ds(first, count)
        self.width = out.shape[-1]
        self.columns = place.columns(self.width)
        self.ready = ready

    def expect(self, index):
        if self.ready is not None:
            pl.semaphore_wait(self.ready.at[self.number, index], 1)

    def stage(self, number):
        p, parts, work, items, width = self.place, self.parts, self.work, self.items, self.width
        first_half, second_half = slice(0, 2 * width), slice(2 * width, 4 * width)
        sides = [slice(side * width, (side + 1) * width) for side in range(4)]
        self.arrive()
        if number == 0:
            self.expect(0)
            for side, column in zip(sides, self.columns[2:]):
                self.send(
                    lambda column=column: parts.at[items, :, :, :, column],
                    lambda side=side: work.at[items, :, :, :, side],
                    p.core_peer,
                )
        elif number == 1:
            for item in self.numbers:
                for side, column in zip(sides, self.columns[:2]):

                    @pl.loop(0, 4)
                    def _(z):
                        work[item, z, :, :, side] += parts[item, z, :, :, column]

            self.expect(1)
            self.send(
                lambda: work.at[items, :, 1 - p.x, :, first_half],
                lambda: work.at[items, :, 0, :, second_half],
                p.x_peer,
            )
        elif number == 2:
            for item in self.numbers:

                @pl.loop(0, 4)
                def _(z):
                    work[item, z, 0, :, second_half] += work[item, z, p.x, :, first_half]

            for step, peer in enumerate(p.z_peers):
                self.expect(3 + step)
                self.send(
                    lambda step=step: work.at[items, p.z_steps[step + 1], 0, :, second_half],
                    lambda step=step: work.at[items, step, 1, :, second_half],
                    peer,
                )
        elif number == 3:
            for item in self.numbers:
                total = work[item, p.z, 0, :, second_half].astype(WIDE)
                for step in range(3):
                    total = total + work[item, step, 1, :, second_half].astype(WIDE)
                work[item, 3, 1, :, second_half] = total.astype(LOW)
            self.expect(2)
            self.send(
                lambda: work.at[items, 3, 1, :, sides[3]],
                lambda: self.last.at[items],
                p.y_peer,
            )
        else:
            for item in self.numbers:
                mine = work[item, 3, 1, :, sides[2]].astype(WIDE)
                self.out[item] = mine + self.last[item].astype(WIDE)


class SumAll(Exchange):
    slots = 5

    def __init__(self, place, values, arrived, sends, recvs):
        super().__init__(sends, recvs, 0)
        p = place
        z_one = p.z + 1 - 2 * lax.rem(p.z, 2)
        peers = (p.core_peer, p.x_peer, p.y_peer, (2 * z_one + p.x, p.tp), p.z_peers[1])
        self.peers, self.values, self.arrived = peers, values, arrived

    def stage(self, number):
        if number:
            self.arrive()
            self.made[-1]().wait_send()
            self.values[...] = self.values[...] + self.arrived[number - 1]
        if number < 5:
            self.send(
                lambda: self.values, lambda: self.arrived.at[number], self.peers[number]
            )


def run_schedule(to, do):
    def step(task, number):
        return lambda: task.stage(number)

    do.fill_self_bias()
    to.place.meet()
    first = [to.keys_values, to.query, to.out, to.bias]
    rest = to.cross + to.ffn
    for task in first + rest:
        task.stage(0)
    for task in (to.embed_row, to.query_row, to.source_row, to.cotangent_row):
        task.start()
    for task in first + rest:
        task.stage(1)
    to.keys_values.stage(2)
    to.query.stage(2)
    to.keys_values.stage(3)
    to.embed_row.near()
    to.query_row.near()
    to.keys_values.stage(4)
    do.near_keys_values()
    to.out.stage(2)
    to.bias.stage(2)
    to.query.stage(3)
    to.query.stage(4)
    do.near_queries()
    to.embed_row.far()
    do.far_keys_values()

    def far_queries():
        to.query_row.far()
        do.far_queries()

    do.attend_self(
        {
            0: [step(to.cross[0], 2), step(to.out, 3)],
            1: [step(to.out, 4), step(to.bias, 3)],
            2: [far_queries, step(to.cross[0], 3), step(to.cross[1], 2)],
            3: [step(to.cross[0], 4), step(to.bias, 4)],
            5: [step(to.ffn[0], 2)],
            7: [step(to.cross[1], 3)],
        }
    )
    do.first_norm()
    to.ffn[1].stage(2)
    to.cross[1].stage(4)
    do.fill_cross_bias()
    do.cross_queries()
    to.source_row.near()
    to.source_row.far()
    do.cross_keys_values()
    do.attend_cross(
        {
            0: [step(to.ffn[0], 3)],
            1: [step(to.ffn[2], 2), step(to.ffn[0], 4)],
            4: [step(to.ffn[1], 3)],
            5: [step(to.ffn[3], 2), step(to.ffn[1], 4)],
        }
    )
    do.bias_in()
    do.feed_forward_in(
        {
            0: [step(to.ffn[2], 3)],
            1: [step(to.ffn[2], 4)],
            2: [step(to.ffn[3], 3)],
        }
    )
    to.cotangent_row.near()
    to.cotangent_row.far()
    to.ffn[3].stage(4)
    do.feed_forward()

    for task in to.ffn:
        task.finish()
    for group in (0, 1):
        for index, peer in enumerate(to.place.summing):
            there = index if index < 3 else 8 - index
            pl.semaphore_signal(
                to.ready.at[group, there], inc=1, device_id=peer, device_id_type=MESH
            )
    to.mixed.give_all()
    do.down_grad()
    to.down_sum.stage(0)
    do.up_grad()
    to.up_sum.stage(0)
    do.cross_out_back()
    to.down_sum.stage(1)
    to.up_sum.stage(1)
    do.cross_back({4: [step(to.down_sum, 2)]})
    do.cross_grads()
    to.cross_sum.stage(0)
    do.source_grad()
    to.source_grad.give_all()
    to.up_sum.stage(2)
    to.cross_sum.stage(1)
    do.first_norm_back()
    to.small_sum.stage(0)
    to.down_sum.stage(3)
    do.self_out_back()
    to.out_sum.stage(0)
    to.small_sum.stage(1)

    def give_query(number):
        def action():
            do.query_grad(number)
            to.query_grad.give(number)

        return action

    do.self_back(
        {
            0: [step(to.out_sum, 1)],
            1: [give_query(0)],
            3: [give_query(1), step(to.cross_sum, 2), step(to.small_sum, 2)],
            4: [step(to.up_sum, 3)],
            5: [give_query(2), step(to.out_sum, 2)],
            7: [give_query(3), step(to.small_sum, 3)],
        }
    )
    to.mixed.wait()
    to.mixed.finish()
    do.key_grad()
    to.key_sum.stage(0)
    do.value_grad()
    to.value_sum.stage(0)
    to.key_sum.stage(1)
    do.query_weight_grad()
    to.query_sum.stage(0)
    to.value_sum.stage(1)
    do.far_embed_grad()
    to.embed_grad.give(0)
    to.embed_grad.give(1)
    to.query_sum.stage(1)
    do.near_embed_grad()
    to.embed_grad.give(2)
    to.embed_grad.give(3)
    to.key_sum.stage(2)
    to.small_sum.stage(4)
    to.value_sum.stage(2)
    to.cross_sum.stage(3)
    to.out_sum.stage(3)
    to.query_sum.stage(2)
    to.down_sum.stage(4)
    to.up_sum.stage(4)
    to.key_sum.stage(3)
    to.value_sum.stage(3)
    to.small_sum.stage(5)
    to.query_sum.stage(3)
    for task in (to.cross_sum, to.out_sum, to.key_sum, to.value_sum, to.query_sum):
        task.stage(4)
    outgoing = [to.source_grad, to.query_grad, to.embed_grad]
    for task in outgoing:
        task.wait()
    for task in outgoing + [to.embed_row, to.query_row, to.source_row, to.cotangent_row]:
        task.finish()
    for task in first + to.cross:
        task.finish()
    for task in (to.down_sum, to.up_sum, to.cross_sum, to.out_sum):
        task.finish()
    for task in (to.key_sum, to.value_sum, to.query_sum):
        task.finish()


def layer_kernel(
    query, embed, source, cotangent, attn_q, attn_k, attn_v, attn_o, cross_q, cross_k, cross_v,
    cross_o, ffn_in, ffn_bias_in, ffn_out, bias_out, norm_gain, norm_bias, lengths, source_lengths,
    rank, limit,
    own_squares, own_wides, small, mixed_blocks, query_blocks, embed_blocks, encoder_blocks, kept_self, kept_cross,
    local_squares, local_wides, local_bias, squares, wides, biases, grad_squares, grad_wides,
    work, last_squares, last_wides, arrived,
    query_row, embed_row, source_row, cotangent_row,
    self_q, self_k, self_v, self_context, other_q, other_k, other_v, other_context,
    flipped, totals, other_totals, inner, highest, normal_one, inverse_one,
    hidden_one, hidden_two, act, pre, grad_ffn, grad_second, key_sum, value_sum, bias, bias_in,
    row_sends, row_recvs, row_own, gather_sends, gather_recvs, gather_own,
    scatter_sends, scatter_recvs, sum_sends, sum_recvs, kept_sems, ready,
):
    place = Place()
    place.greet()
    row = place.tp
    length, features = query_row.shape
    hidden = act.shape[1]
    half = length // 2
    near_half, far_half = rows_of(place.y, half), rows_of(1 - place.y, half)

    for index, piece in enumerate((attn_q, attn_k, attn_v, attn_o, cross_q, cross_k, cross_v, cross_o)):
        local_squares[index] = piece[...]
    local_wides[0] = ffn_in[...]
    local_wides[1] = ffn_out[...]
    local_bias[...] = jnp.zeros_like(local_bias)
    local_bias[0, 0:1, 0:64] = ffn_bias_in[...]
    small[...] = jnp.zeros_like(small)
    flipped[:, 64:] = jnp.ones((HEADS, flipped.shape[1] - 64, length), LOW)

    def gather(number, local, full, first, count, side=0, sides=1):
        sems = (gather_sends, gather_recvs, gather_own)
        return Gather(place, local, full, first, count, side, sides, *sems, number)

    def scatter(number, *buffers):
        return Scatter(place, *buffers, scatter_sends, scatter_recvs, number)

    def row_sems(number):
        return row_sends, row_recvs, row_own, number

    def square(index):
        return squares[index].reshape(features, features)

    def wide(index):
        return wides[index].reshape(features, hidden)

    def vector(index):
        first = (index % 4) * features
        return small.at[1 + index // 4 : 2 + index // 4, first : first + features]

    def quarter(ref, index):
        return ref.at[:, index * features : (index + 1) * features]

    square_sums = (grad_squares, work, last_squares, own_squares)
    wide_sums = (grad_wides, wides, last_wides, own_wides)
    to = SimpleNamespace(
        place=place,
        ready=ready,
        keys_values=gather(0, local_squares, squares, 1, 2),
        query=gather(1, local_squares, squares, 0, 1),
        out=gather(2, local_squares, squares, 3, 1),
        cross=[gather(3 + i, local_squares, squares, 4 + 2 * i, 2) for i in (0, 1)],
        ffn=[gather(5 + i, local_wides, wides, i // 2, 1, i % 2, 2) for i in range(4)],
        bias=gather(9, local_bias, biases, 0, 1),
        embed_row=ToRow(place, embed, embed_row, *row_sems(0)),
        query_row=ToRow(place, query, query_row, *row_sems(1)),
        source_row=ToRow(place, source, source_row, *row_sems(2)),
        cotangent_row=ToRow(place, cotangent, cotangent_row, *row_sems(3)),
        down_sum=scatter(0, *wide_sums, 1, 1, ready),
        up_sum=scatter(1, *wide_sums, 0, 1, ready),
        cross_sum=scatter(2, *square_sums, 4, 4, None),
        out_sum=scatter(3, *square_sums, 3, 1, None),
        key_sum=scatter(4, *square_sums, 1, 1, None),
        value_sum=scatter(5, *square_sums, 2, 1, None),
        query_sum=scatter(6, *square_sums, 0, 1, None),
        small_sum=SumAll(place, small, arrived, sum_sends, sum_recvs),
        mixed=FromRow(place, cotangent_row, mixed_blocks, *row_sems(4)),
        source_grad=FromRow(place, source_row, encoder_blocks, *row_sems(5)),
        query_grad=FromRow(place, hidden_two, query_blocks, *row_sems(6)),
        embed_grad=FromRow(place, cotangent_row, embed_blocks, *row_sems(7)),
    )
    score_room = ((key_sum, value_sum), highest)
    cotangent_low, grad_k, grad_v, grad_q = (quarter(act, i) for i in range(4))
    room = tuple(quarter(bias, i) for i in (0, 1))

    def fill_keys_values(rows):
        self_k[rows] = nn(embed_row[rows], square(1)).astype(LOW)
        self_v[rows] = nn(embed_row[rows], square(2)).astype(LOW)

    def fill_queries(rows):
        self_q[rows] = (nn(query_row[rows], square(0)) * 0.125).astype(LOW)

    def turned(step):
        return (length // Q_TILE - 1 - step // PAIRS) * PAIRS + lax.rem(step, PAIRS)

    def attend_self(after):
        flip_heads(self_v, flipped)
        attend(
            self_k, self_q, flipped, bias, self_context, totals,
            lambda number: place.tile(3 - number), score_room, Kept(kept_self, act, kept_sems, turned), after,
        )

    def first_norm():
        @pl.loop(0, length // 256)
        def _(tile):
            part = rows_of(tile, 256)
            branch = nt(self_context[part], square(3))
            normal, inverse = normalize(query_row[part].astype(WIDE) + branch)
            normal_one[part] = normal
            inverse_one[part] = inverse
            hidden_one[part] = (normal * norm_gain[0:1] + norm_bias[0:1]).astype(LOW)

    def fill_cross_queries():
        other_q[...] = (nn(hidden_one[...], square(4)) * 0.125).astype(LOW)

    def fill_cross_keys_values():
        other_k[...] = nn(source_row[...], square(5)).astype(LOW)
        other_v[...] = nn(source_row[...], square(6)).astype(LOW)

    def attend_cross(after):
        flip_heads(other_v, flipped)
        attend(
            other_k, other_q, flipped, bias, other_context, other_totals,
            lambda number: number, score_room, Kept(kept_cross, act, kept_sems), after,
        )

    def fill_bias_in():
        for block in range(4):
            pieces = biases[0, :, :, :, block * 128 : block * 128 + 128].reshape(128, 128)
            size = hidden // 4
            lane = lax.broadcasted_iota(jnp.int32, (128, size), 1)
            line = lax.broadcasted_iota(jnp.int32, (128, size), 0)
            spread = nn(pieces, jnp.where(lane % 64 == line, 1.0, 0.0).astype(LOW))
            spread = jnp.where(lane // 64 == line // 16, spread, 0.0)
            bias_in[:, block * size : block * size + size] = jnp.sum(spread, axis=0, keepdims=True)

    def feed_forward_in(after):
        @pl.loop(0, length // 256)
        def _(tile):
            part = rows_of(tile, 256)
            branch = nt(other_context[part], square(7))
            before = normal_one[part] * norm_gain[0:1] + norm_bias[0:1]
            normal, inverse = normalize(before + branch)
            grad_second[part] = normal
            key_sum[part, 0:1] = inverse
            low = (normal * norm_gain[1:2] + norm_bias[1:2]).astype(LOW)
            hidden_two[part] = low
            before = nn(low, wide(0)) + bias_in[...]
            below = 0.5 * (1.0 + lax.erf(before * 0.7071067811865476))
            density = jnp.exp(-0.5 * before * before) * 0.3989422804014327
            pre[part] = (below + before * density).astype(LOW)
            act[part] = (before * below).astype(LOW)
            run_after(tile, after)

    def feed_forward():
        @pl.loop(0, length // 256)
        def _(tile):
            part = rows_of(tile, 256)
            normal_mid = grad_second[part]
            after = normal_mid * norm_gain[1:2] + norm_bias[1:2]
            after = after + nt(act[part], wide(1)) + bias_out[...]
            normal, inverse = normalize(after)
            grad = cotangent_row[part].astype(WIDE)
            cotangent_row[part] = (normal * norm_gain[2:3] + norm_bias[2:3]).astype(LOW)
            add_rows(vector(2), grad * normal)
            add_rows(vector(5), grad)
            grad = normalize_back(grad, normal, inverse, norm_gain[2:3])
            low = grad.astype(LOW)
            grad_ffn[part] = low
            add_rows(vector(6), low.astype(WIDE))
            grad_pre = (nn(low, wide(1)) * pre[part].astype(WIDE)).astype(LOW)
            pre[part] = grad_pre
            add_rows(small.at[0:1], grad_pre.astype(WIDE))
            grad = grad + nt(grad_pre, wide(0))
            add_rows(vector(1), grad * normal_mid)
            add_rows(vector(4), grad)
            inverse_mid = key_sum[part, 0:1]
            grad_second[part] = normalize_back(grad, normal_mid, inverse_mid, norm_gain[1:2])

    def wide_grad(index, left, right):
        for side in (slice(0, hidden // 2), slice(hidden // 2, hidden)):
            total = tn(left[...], right[:, side]).astype(LOW)
            grad_wides[index, :, :, :, side] = total.reshape(4, 2, features // 8, hidden // 2)

    def square_grad(index, inputs, grad):
        grad_squares[index] = tn(inputs, grad).astype(LOW).reshape(grad_squares.shape[1:])

    def out_back(first, context, inverses, kept):
        for index in range(4):
            Kept(kept, pre, kept_sems).load(index).start()
        grad = grad_second[...].astype(LOW)
        square_grad(first + 3, grad, context[...])
        lane = lax.broadcasted_iota(jnp.int32, (HEADS, features), 1)
        head = lax.broadcasted_iota(jnp.int32, (HEADS, features), 0)
        spread = lax.dot_general(
            inverses[...],
            jnp.where(lane // 64 == head, 1.0, 0.0),
            (((0,), (0,)), ((), ())),
            precision=lax.Precision.HIGHEST,
            preferred_element_type=WIDE,
        )
        cotangent_low[...] = (nn(grad, square(first + 3)) * spread).astype(LOW)

    def attend_back_with(keys, queries, values, context, kept, tile_of, after):
        flip_heads(keys, flipped)
        inner_products(cotangent_low, context, inner)
        attend_back(
            flipped, queries, values, cotangent_low, inner,
            (key_sum, value_sum, grad_q), tile_of, room, Kept(kept, pre, kept_sems), after,
        )
        grad_k[...] = key_sum[...].astype(LOW)
        grad_v[...] = value_sum[...].astype(LOW)

    def cross_grads():
        square_grad(4, hidden_one[...], grad_q[...])
        square_grad(5, source_row[...], grad_k[...])
        square_grad(6, source_row[...], grad_v[...])

    def fill_source_grad():
        source_row[...] = (nt(grad_k[...], square(5)) + nt(grad_v[...], square(6))).astype(LOW)

    def first_norm_back():
        @pl.loop(0, length // 256)
        def _(tile):
            part = rows_of(tile, 256)
            grad = grad_second[part] + nt(grad_q[part], square(4))
            normal = normal_one[part]
            add_rows(vector(0), grad * normal)
            add_rows(vector(3), grad)
            grad_second[part] = normalize_back(grad, normal, inverse_one[part], norm_gain[0:1])

    def fill_query_grad(number):
        part = rows_of(place.tile(number), Q_TILE)
        grad = grad_second[part] + nt(grad_q[part], square(0))
        hidden_two[part] = grad.astype(LOW)

    def fill_embed_grad(rows):
        grad = nt(grad_k[rows], square(1)) + nt(grad_v[rows], square(2))
        cotangent_row[rows] = grad.astype(LOW)

    run_schedule(
        to,
        SimpleNamespace(
            fill_self_bias=lambda: fill_self_bias(bias, lengths, rank, limit, row),
            fill_cross_bias=lambda: fill_cross_bias(bias, lengths, source_lengths, row),
            near_keys_values=lambda: fill_keys_values(near_half),
            far_keys_values=lambda: fill_keys_values(far_half),
            near_queries=lambda: fill_queries(near_half),
            far_queries=lambda: fill_queries(far_half),
            attend_self=attend_self,
            first_norm=first_norm,
            cross_queries=fill_cross_queries,
            cross_keys_values=fill_cross_keys_values,
            attend_cross=attend_cross,
            bias_in=fill_bias_in,
            feed_forward_in=feed_forward_in,
            feed_forward=feed_forward,
            down_grad=lambda: wide_grad(1, grad_ffn, act),
            up_grad=lambda: wide_grad(0, hidden_two, pre),
            cross_out_back=lambda: out_back(4, other_context, other_totals, kept_cross),
            cross_back=lambda after: attend_back_with(
                other_k, other_q, other_v, other_context, kept_cross, lambda number: number, after
            ),
            cross_grads=cross_grads,
            source_grad=fill_source_grad,
            first_norm_back=first_norm_back,
            self_out_back=lambda: out_back(0, self_context, totals, kept_self),
            self_back=lambda after: attend_back_with(
                self_k, self_q, self_v, self_context, kept_self, place.tile, after
            ),
            query_grad=fill_query_grad,
            far_embed_grad=lambda: fill_embed_grad(far_half),
            near_embed_grad=lambda: fill_embed_grad(near_half),
            key_grad=lambda: square_grad(1, embed_row[...], grad_k[...]),
            value_grad=lambda: square_grad(2, embed_row[...], grad_v[...]),
            query_weight_grad=lambda: square_grad(0, query_row[...], grad_q[...]),
        ),
    )


def run_layer(streams, weights, vectors, tables):
    _, size, features = streams[0].shape
    length = 4 * size
    hidden = 4 * weights[8].shape[1]
    shape = jax.ShapeDtypeStruct
    vmem_in = pl.BlockSpec(memory_space=pltpu.VMEM)
    smem_in = pl.BlockSpec(memory_space=pltpu.SMEM)
    hbm = pl.BlockSpec(memory_space=pl.ANY)
    vmem, dma = pltpu.VMEM, pltpu.SemaphoreType.DMA
    row, wide_row = vmem((length, features), LOW), vmem((length, features), WIDE)
    per_head, column = vmem((HEADS, length), WIDE), vmem((length, 1), WIDE)
    full_squares = vmem((8, 4, 2, features // 8, features), LOW)
    full_wides = vmem((2, 4, 2, features // 8, hidden), LOW)
    blocks = shape((4, size, features), LOW)
    return pl.pallas_call(
        layer_kernel,
        out_shape=[
            shape((8, features // 8, features // 4), WIDE),
            shape((2, features // 8, hidden // 4), WIDE),
            shape((8, hidden), WIDE),
        ]
        + [blocks] * 4
        + [shape((length // Q_TILE * PAIRS, length, 2 * Q_TILE), LOW)] * 2,
        in_specs=[hbm] * 4 + [vmem_in] * 14 + [smem_in] * 2 + [vmem_in] * 2,
        out_specs=[vmem_in] * 3 + [hbm] * 6,
        scratch_shapes=[
            vmem((8, features // 8, features // 4), LOW),
            vmem((2, features // 8, hidden // 4), LOW),
            vmem((1, 16, 128), LOW),
            full_squares,
            full_wides,
            vmem((1, 4, 2, 16, 512), LOW),
            full_squares,
            full_wides,
            full_squares,
            vmem((8, features // 8, features // 4), LOW),
            vmem((2, features // 8, hidden // 4), LOW),
            vmem((5, 8, hidden), WIDE),
        ]
        + [row] * 12
        + [vmem((HEADS, 80, length), LOW)]
        + [per_head] * 3
        + [vmem((4, 1, Q_TILE), WIDE)]
        + [wide_row, column, row, row]
        + [vmem((length, hidden), LOW)] * 2
        + [row, wide_row, wide_row, wide_row, vmem((length, length), LOW)]
        + [vmem((1, hidden), WIDE)]
        + [dma((8, 3)), dma((8, 3)), dma((8,))]
        + [dma((10, Gather.slots)), dma((10, Gather.slots)), dma((10,))]
        + [dma((7, Scatter.slots)), dma((7, Scatter.slots)), dma((1, 5)), dma((1, 5)), dma((4,))]
        + [pltpu.SemaphoreType.REGULAR((2, 6))],
        compiler_params=pltpu.CompilerParams(
            collective_id=0, has_side_effects=True, vmem_limit_bytes=127 * 2**19
        ),
        name="layer",
    )(*streams, *weights, *vectors, *tables)[:7]


def outputs_kernel(
    squares, wides, small, mixed, grad_query, grad_embed, grad_encoder,
    mixed_out, query_out, embed_out, encoder_out, *rest,
):
    square_outs, wide_outs, (bias_in, bias_out, gains, shifts) = rest[:8], rest[8:10], rest[10:]
    mixed_out[...] = mixed[...]
    for low, out in ((grad_query, query_out), (grad_embed, embed_out), (grad_encoder, encoder_out)):
        out[...] = low[...].astype(WIDE)

    @pl.when(pl.program_id(0) == 0)
    def _():
        for index, out in enumerate(square_outs):
            out[...] = squares[index]
        for index, out in enumerate(wide_outs):
            out[...] = wides[index]
        features = gains.shape[1]
        for index in range(7):
            first = (index % 4) * features
            value = small[1 + index // 4 : 2 + index // 4, first : first + features]
            if index == 6:
                bias_out[...] = value
            else:
                (gains if index < 3 else shifts)[index % 3 : index % 3 + 1] = value
        count = wides.shape[2]
        mine = small[0:1, rows_of(lax.axis_index("tp"), count)]
        shift = lax.rem(count - lax.axis_index("dp") * bias_in.shape[1], count)
        bias_in[...] = pltpu.roll(mine, shift, 1)[:, : bias_in.shape[1]]


def write_outputs(squares, wides, small, *blocks):
    shape = jax.ShapeDtypeStruct
    rows, size, features = blocks[0].shape
    whole = pl.BlockSpec(memory_space=pltpu.VMEM)
    one = pl.BlockSpec((1, size, features), lambda i: (i, 0, 0))

    def fixed(extent):
        return pl.BlockSpec(extent, lambda i: (0,) * len(extent))

    singles = [squares.shape[1:]] * 8 + [wides.shape[1:]] * 2
    singles += [(1, wides.shape[1]), (1, features), (3, features), (3, features)]
    return pl.pallas_call(
        outputs_kernel,
        grid=(rows,),
        out_shape=[shape(blocks[0].shape, LOW)]
        + [shape(blocks[0].shape, WIDE)] * 3
        + [shape(extent, WIDE) for extent in singles],
        in_specs=[fixed(squares.shape), fixed(wides.shape), fixed(small.shape)] + [one] * 4,
        out_specs=[one] * 4 + [fixed(extent) for extent in singles],
        name="outputs",
    )(squares, wides, small, *blocks)


def local_rows(
    query_stream,
    token_embed,
    encoder_out,
    out_grad,
    attn_q,
    attn_k,
    attn_v,
    attn_o,
    cross_q,
    cross_k,
    cross_v,
    cross_o,
    ffn_in,
    ffn_bias_in,
    ffn_out,
    ffn_bias_out,
    norm_gain,
    norm_bias,
    doc_lengths,
    src_lengths,
    ctx_rank,
    ctx_limit,
):
    received = run_layer(
        (query_stream, token_embed, encoder_out, out_grad),
        (attn_q, attn_k, attn_v, attn_o.T, cross_q, cross_k, cross_v, cross_o.T)
        + (ffn_in, ffn_bias_in[None], ffn_out.T),
        (ffn_bias_out[None], norm_gain, norm_bias),
        (doc_lengths, src_lengths, ctx_rank, ctx_limit),
    )
    (
        mixed,
        grad_query,
        grad_embed,
        grad_encoder,
        grad_attn_q,
        grad_attn_k,
        grad_attn_v,
        grad_attn_o,
        grad_cross_q,
        grad_cross_k,
        grad_cross_v,
        grad_cross_o,
        grad_ffn_in,
        grad_ffn_out,
        grad_bias_in,
        grad_bias_out,
        gain_grads,
        shift_grads,
    ) = write_outputs(*received)
    return (
        mixed,
        grad_query,
        grad_embed,
        grad_encoder,
        grad_attn_q,
        grad_attn_k,
        grad_attn_v,
        grad_attn_o.T,
        grad_cross_q,
        grad_cross_k,
        grad_cross_v,
        grad_cross_o.T,
        grad_ffn_in,
        grad_bias_in[0],
        grad_ffn_out.T,
        grad_bias_out[0],
        gain_grads,
        shift_grads,
    )


def local(*arrays):
    if arrays[0].shape[0] == 4 and (lax.axis_size("dp"), lax.axis_size("tp")) == (8, 4):
        return local_rows(*arrays)
    return local_split(*arrays)


def solution(mesh):
    in_specs = (
        P("dp", "tp", None),
        P("dp", "tp", None),
        P("dp", "tp", None),
        P("dp", "tp", None),
        P("dp", "tp"),
        P("dp", "tp"),
        P("dp", "tp"),
        P("tp", "dp"),
        P("dp", "tp"),
        P("dp", "tp"),
        P("dp", "tp"),
        P("tp", "dp"),
        P("dp", "tp"),
        P(("tp", "dp")),
        P("tp", "dp"),
        P(),
        P(),
        P(),
        P("dp", None),
        P("dp", None),
        P("dp", None),
        P("dp", None),
    )
    out_specs = (
        P("dp", "tp", None),
        P("dp", "tp", None),
        P("dp", "tp", None),
        P("dp", "tp", None),
        P("dp", "tp"),
        P("dp", "tp"),
        P("dp", "tp"),
        P("tp", "dp"),
        P("dp", "tp"),
        P("dp", "tp"),
        P("dp", "tp"),
        P("tp", "dp"),
        P("dp", "tp"),
        P(("tp", "dp")),
        P("tp", "dp"),
        P(),
        P(),
        P(),
    )
    return jax.shard_map(local, mesh=mesh, in_specs=in_specs, out_specs=out_specs, check_vma=False)
```

profile of v0, /device:TPU:0, one launch (start us, length us, event | category | flops | bytes accessed | tf_op | source)
XLA Modules:
  0.0 201.7 jit_solution(17873891774322761717)
XLA Ops:
  0.7 194.7 %layer.1 = (f32[8,64,128]{2,1,0:T(8,128)}, f32[2,64,512]{2,1,0:T(8,128)}, f32[8,2048]{1,0:T(8,128)}, bf16[4,256,512]{2,1,0:T(8,128)(2,1)}, bf16[4,256,512]{2,1,0...) custom-call(bf16[4,256,512]{2,1,0:T(8,128)(2,1)} %query.1, ...), custom_call_target="tpu_custom_call" | custom-call | tf_op jit(solution)/shard_map/layer/pallas_call | solution.py:1404
  195.3 6.2 %outputs.1 = (bf16[4,256,512]{2,1,0:T(8,128)(2,1)}, f32[4,256,512]{2,1,0:T(8,128)}, f32[4,256,512]{2,1,0:T(8,128)}, f32[4,256,512]{2,1,0:T(8,128)}, f32[64,128]{...) custom-call(f32[8,64,128]{2,1,0:T(8,128)} %get-tuple-element.43.squa, ...), custom_call_target="tpu_custom_call" | custom-call | tf_op jit(solution)/shard_map/outputs/pallas_call | solution.py:1488
where the time goes:
time: 205 us; the launch traced here: 202 us
  Pallas kernels  201 us (98%)
    pallas_call x1, Pallas kernels, run_layer(): pl.pallas_call(layer_kernel, out_shape=[shape((8, features // 8, features...  195 us
    pallas_call x1, Pallas kernels, write_outputs(): pl.pallas_call(outputs_kernel, grid=(rows,), out_shape=[shape(blocks[0].s...  6.16 us

commit v1 on v0

--- a/solution.py
+++ b/solution.py
@@ -859,6 +859,16 @@
         self.columns = place.columns(self.width)
         self.ready = ready
 
+    def add_core(self):
+        width = self.width
+        for item in self.numbers:
+            for side in (0, 1):
+
+                @pl.loop(0, 4)
+                def _(z):
+                    mine = self.parts[item, z, :, :, self.columns[side]]
+                    self.work[item, z, :, :, side * width : (side + 1) * width] += mine
+
     def expect(self, index):
         if self.ready is not None:
             pl.semaphore_wait(self.ready.at[self.number, index], 1)
@@ -877,13 +887,7 @@
                     p.core_peer,
                 )
         elif number == 1:
-            for item in self.numbers:
-                for side, column in zip(sides, self.columns[:2]):
-
-                    @pl.loop(0, 4)
-                    def _(z):
-                        work[item, z, :, :, side] += parts[item, z, :, :, column]
-
+            self.add_core()
             self.expect(1)
             self.send(
                 lambda: work.at[items, :, 1 - p.x, :, first_half],
@@ -922,6 +926,50 @@
                 self.out[item] = mine + self.last[item].astype(WIDE)
 
 
+class ScatterAcross(Scatter):
+    def __init__(
+        self, place, parts, work, last, out, first, count, ready, across, sends, recvs, number
+    ):
+        super().__init__(place, parts, work, last, out, first, count, ready, sends, recvs, number)
+        self.across = across
+
+    def stage(self, number):
+        if number == 0:
+            super().stage(0)
+            return
+        p, work, items, width = self.place, self.work, self.items, self.width
+        first_half, second_half = slice(0, 2 * width), slice(2 * width, 4 * width)
+        kept, given = slice(2 * width, 3 * width), slice(3 * width, 4 * width)
+        self.arrive()
+        if number == 1:
+            self.add_core()
+            for step, peer in enumerate(p.z_peers):
+                self.send(
+                    lambda step=step: work.at[items, p.z_steps[step + 1], :, :, first_half],
+                    lambda step=step: work.at[items, step, :, :, second_half],
+                    peer,
+                )
+        elif number == 2:
+            for item in self.numbers:
+                total = work[item, p.z, :, :, first_half].astype(WIDE)
+                for step in range(3):
+                    total = total + work[item, step, :, :, second_half].astype(WIDE)
+                work[item, 3, :, :, second_half] = total.astype(LOW)
+            self.send(
+                lambda: work.at[items, 3, 1 - p.x, :, second_half], lambda: self.across, p.x_peer
+            )
+        elif number == 3:
+            for item in self.numbers:
+                work[item, 3, p.x, :, second_half] += self.across[0]
+            self.send(
+                lambda: work.at[items, 3, p.x, :, given], lambda: self.last.at[items], p.y_peer
+            )
+        else:
+            for item in self.numbers:
+                mine = work[item, 3, p.x, :, kept].astype(WIDE)
+                self.out[item] = mine + self.last[item].astype(WIDE)
+
+
 class SumAll(Exchange):
     slots = 5
 
@@ -951,11 +999,17 @@
     to.place.meet()
     first = [to.keys_values, to.query, to.out, to.bias]
     rest = to.cross + to.ffn
-    for task in first + rest:
+    for task in first + to.cross:
         task.stage(0)
-    for task in (to.embed_row, to.query_row, to.source_row, to.cotangent_row):
-        task.start()
-    for task in first + rest:
+    to.embed_row.start()
+    for task in to.ffn[:2]:
+        task.stage(0)
+    to.query_row.start()
+    for task in to.ffn[2:]:
+        task.stage(0)
+    to.source_row.start()
+    to.cotangent_row.start()
+    for task in first + to.cross:
         task.stage(1)
     to.keys_values.stage(2)
     to.query.stage(2)
@@ -971,6 +1025,8 @@
     do.near_queries()
     to.embed_row.far()
     do.far_keys_values()
+    for task in to.ffn[:2]:
+        task.stage(1)
 
     def far_queries():
         to.query_row.far()
@@ -980,7 +1036,7 @@
         {
             0: [step(to.cross[0], 2), step(to.out, 3)],
             1: [step(to.out, 4), step(to.bias, 3)],
-            2: [far_queries, step(to.cross[0], 3), step(to.cross[1], 2)],
+            2: [far_queries, step(to.ffn[2], 1), step(to.ffn[3], 1), step(to.cross[0], 3), step(to.cross[1], 2)],
             3: [step(to.cross[0], 4), step(to.bias, 4)],
             5: [step(to.ffn[0], 2)],
             7: [step(to.cross[1], 3)],
@@ -996,16 +1052,15 @@
     do.cross_keys_values()
     do.attend_cross(
         {
-            0: [step(to.ffn[0], 3)],
-            1: [step(to.ffn[2], 2), step(to.ffn[0], 4)],
-            4: [step(to.ffn[1], 3)],
-            5: [step(to.ffn[3], 2), step(to.ffn[1], 4)],
+            0: [step(to.ffn[2], 2), step(to.ffn[0], 3)],
+            3: [step(to.ffn[3], 2), step(to.ffn[0], 4), step(to.ffn[1], 3)],
+            5: [step(to.ffn[1], 4)],
+            7: [step(to.ffn[2], 3)],
         }
     )
     do.bias_in()
     do.feed_forward_in(
         {
-            0: [step(to.ffn[2], 3)],
             1: [step(to.ffn[2], 4)],
             2: [step(to.ffn[3], 3)],
         }
@@ -1064,14 +1119,14 @@
     )
     to.mixed.wait()
     to.mixed.finish()
+    do.value_grad()
+    to.value_sum.stage(0)
     do.key_grad()
     to.key_sum.stage(0)
-    do.value_grad()
-    to.value_sum.stage(0)
-    to.key_sum.stage(1)
+    to.value_sum.stage(1)
     do.query_weight_grad()
     to.query_sum.stage(0)
-    to.value_sum.stage(1)
+    to.key_sum.stage(1)
     do.far_embed_grad()
     to.embed_grad.give(0)
     to.embed_grad.give(1)
@@ -1081,16 +1136,16 @@
     to.embed_grad.give(3)
     to.key_sum.stage(2)
     to.small_sum.stage(4)
+    to.query_sum.stage(2)
     to.value_sum.stage(2)
     to.cross_sum.stage(3)
     to.out_sum.stage(3)
-    to.query_sum.stage(2)
     to.down_sum.stage(4)
     to.up_sum.stage(4)
     to.key_sum.stage(3)
-    to.value_sum.stage(3)
     to.small_sum.stage(5)
     to.query_sum.stage(3)
+    to.value_sum.stage(3)
     for task in (to.cross_sum, to.out_sum, to.key_sum, to.value_sum, to.query_sum):
         task.stage(4)
     outgoing = [to.source_grad, to.query_grad, to.embed_grad]
@@ -1112,7 +1167,7 @@
     rank, limit,
     own_squares, own_wides, small, mixed_blocks, query_blocks, embed_blocks, encoder_blocks, kept_self, kept_cross,
     local_squares, local_wides, local_bias, squares, wides, biases, grad_squares, grad_wides,
-    work, last_squares, last_wides, arrived,
+    work, last_squares, last_wides, arrived, across,
     query_row, embed_row, source_row, cotangent_row,
     self_q, self_k, self_v, self_context, other_q, other_k, other_v, other_context,
     flipped, totals, other_totals, inner, highest, normal_one, inverse_one,
@@ -1142,7 +1197,8 @@
         return Gather(place, local, full, first, count, side, sides, *sems, number)
 
     def scatter(number, *buffers):
-        return Scatter(place, *buffers, scatter_sends, scatter_recvs, number)
+        kind = Scatter if len(buffers) == 7 else ScatterAcross
+        return kind(place, *buffers, scatter_sends, scatter_recvs, number)
 
     def row_sems(number):
         return row_sends, row_recvs, row_own, number
@@ -1180,7 +1236,7 @@
         cross_sum=scatter(2, *square_sums, 4, 4, None),
         out_sum=scatter(3, *square_sums, 3, 1, None),
         key_sum=scatter(4, *square_sums, 1, 1, None),
-        value_sum=scatter(5, *square_sums, 2, 1, None),
+        value_sum=scatter(5, *square_sums, 2, 1, None, across),
         query_sum=scatter(6, *square_sums, 0, 1, None),
         small_sum=SumAll(place, small, arrived, sum_sends, sum_recvs),
         mixed=FromRow(place, cotangent_row, mixed_blocks, *row_sems(4)),
@@ -1425,6 +1481,7 @@
             vmem((8, features // 8, features // 4), LOW),
             vmem((2, features // 8, hidden // 4), LOW),
             vmem((5, 8, hidden), WIDE),
+            vmem((1, features // 8, features // 2), LOW),
         ]
         + [row] * 12
         + [vmem((HEADS, 80, length), LOW)]

time: 205 us -> 199 us (0.971)
  Pallas kernels: 201 us -> 194 us
    pallas_call x1, Pallas kernels: 195 us -> 188 us  [run_layer(): pl.pallas_call(layer_kernel, out_shape=[shape((8, features // 8, features...]
where the time goes in v1:
time: 199 us; the launch traced here: 195 us
  Pallas kernels  194 us (97%)
    pallas_call x1, Pallas kernels, run_layer(): pl.pallas_call(layer_kernel, out_shape=[shape((8, features // 8, features...  188 us
    pallas_call x1, Pallas kernels, write_outputs(): pl.pallas_call(outputs_kernel, grid=(rows,), out_shape=[shape(blocks[0].s...  6.16 us

profile of v1, /device:TPU:0, one launch (start us, length us, event | category | flops | bytes accessed | tf_op | source)
XLA Modules:
  0.0 195.3 jit_solution(12059971154879691576)
XLA Ops:
  0.7 188.3 %layer.1 = (f32[8,64,128]{2,1,0:T(8,128)}, f32[2,64,512]{2,1,0:T(8,128)}, f32[8,2048]{1,0:T(8,128)}, bf16[4,256,512]{2,1,0:T(8,128)(2,1)}, bf16[4,256,512]{2,1,0...) custom-call(bf16[4,256,512]{2,1,0:T(8,128)(2,1)} %query.1, ...), custom_call_target="tpu_custom_call" | custom-call | tf_op jit(solution)/shard_map/layer/pallas_call | solution.py:1460
  188.9 6.2 %outputs.1 = (bf16[4,256,512]{2,1,0:T(8,128)(2,1)}, f32[4,256,512]{2,1,0:T(8,128)}, f32[4,256,512]{2,1,0:T(8,128)}, f32[4,256,512]{2,1,0:T(8,128)}, f32[64,128]{...) custom-call(f32[8,64,128]{2,1,0:T(8,128)} %get-tuple-element.43.squa, ...), custom_call_target="tpu_custom_call" | custom-call | tf_op jit(solution)/shard_map/outputs/pallas_call | solution.py:1545

commit v2 on v1

--- a/solution.py
+++ b/solution.py
@@ -471,8 +471,8 @@
     target[...] += jnp.sum(grad, axis=0, keepdims=True)
 
 
-def documents(lengths, row, shape, axis):
-    positions = lax.broadcasted_iota(jnp.int32, shape, axis)
+def documents(lengths, row, shape, axis, first=0):
+    positions = lax.broadcasted_iota(jnp.int32, shape, axis) + first
     document = jnp.full(shape, -1, jnp.int32)
     start = jnp.zeros(shape, jnp.int32)
     offset = jnp.int32(0)
@@ -487,24 +487,28 @@
 def fill_self_bias(bias, lengths, rank, limit, row):
     length = bias.shape[0]
     key_position, key_document, _ = documents(lengths, row, (length, 1), 0)
-    position, document, start = documents(lengths, row, (1, length), 1)
     rank_row = rank[pl.ds(row, 1), :].astype(WIDE)
     key_rank = jnp.transpose(jnp.broadcast_to(rank_row, (128, length)))[:, :1]
-    query_limit = limit[pl.ds(row, 1), :].astype(WIDE)
-    for tile in range(length // Q_TILE):
-        part = slice(tile * Q_TILE, (tile + 1) * Q_TILE)
-        chosen = (key_rank < query_limit[:, part]) & (key_position != position[:, part])
-        seen = (key_document == document[:, part]) & (chosen | (key_position == start[:, part]))
+
+    @pl.loop(0, length // Q_TILE)
+    def _(tile):
+        part = rows_of(tile, Q_TILE)
+        position, document, start = documents(lengths, row, (1, Q_TILE), 1, tile * Q_TILE)
+        query_limit = limit[pl.ds(row, 1), part].astype(WIDE)
+        chosen = (key_rank < query_limit) & (key_position != position)
+        seen = (key_document == document) & (chosen | (key_position == start))
         bias[:, part] = jnp.where(seen, 0.0, HIDDEN).astype(bias.dtype)
 
 
 def fill_cross_bias(bias, lengths, source_lengths, row):
     length = bias.shape[0]
     _, key_document, _ = documents(source_lengths, row, (length, 1), 0)
-    _, document, _ = documents(lengths, row, (1, length), 1)
-    for tile in range(length // Q_TILE):
-        part = slice(tile * Q_TILE, (tile + 1) * Q_TILE)
-        seen = key_document == document[:, part]
+
+    @pl.loop(0, length // Q_TILE)
+    def _(tile):
+        part = rows_of(tile, Q_TILE)
+        _, document, _ = documents(lengths, row, (1, Q_TILE), 1, tile * Q_TILE)
+        seen = key_document == document
         bias[:, part] = jnp.where(seen, 0.0, HIDDEN).astype(bias.dtype)
 
 
@@ -656,20 +660,29 @@
 
 
 def inner_products(cotangent, context, inner):
-    products = cotangent[...].astype(WIDE) * context[...].astype(WIDE)
-    high = products.astype(LOW)
-    rest = (products - high.astype(WIDE)).astype(LOW)
-    shape = (2 * HEADS, products.shape[1])
+    length, features = cotangent.shape
+    shape = (2 * HEADS, features)
     head = lax.broadcasted_iota(jnp.int32, shape, 0)
     lane = lax.broadcasted_iota(jnp.int32, shape, 1)
     pick = jnp.where(lane // 64 == head, 1.0, 0.0).astype(LOW)
-    inner[...] = (nt(pick, high) + nt(pick, rest))[:HEADS]
+
+    @pl.loop(0, 2)
+    def _(tile):
+        part = rows_of(tile, length // 2)
+        products = cotangent[part].astype(WIDE) * context[part].astype(WIDE)
+        high = products.astype(LOW)
+        rest = (products - high.astype(WIDE)).astype(LOW)
+        inner[:, part] = (nt(pick, high) + nt(pick, rest))[:HEADS]
 
 
 def flip_heads(values, flipped):
-    turned = jnp.transpose(values[...])
-    for head in range(HEADS):
-        flipped[head, :64] = turned[64 * head : 64 * head + 64]
+    @pl.loop(0, 2)
+    def _(tile):
+        part = rows_of(tile, values.shape[0] // 2)
+        turned = jnp.transpose(values[part])
+        for head in range(HEADS):
+            flipped[head, :64, part] = turned[64 * head : 64 * head + 64]
+
 
 MESH = pl.DeviceIdType.MESH
 
@@ -1276,11 +1289,17 @@
             hidden_one[part] = (normal * norm_gain[0:1] + norm_bias[0:1]).astype(LOW)
 
     def fill_cross_queries():
-        other_q[...] = (nn(hidden_one[...], square(4)) * 0.125).astype(LOW)
+        @pl.loop(0, 2)
+        def _(tile):
+            rows = rows_of(tile, half)
+            other_q[rows] = (nn(hidden_one[rows], square(4)) * 0.125).astype(LOW)
 
     def fill_cross_keys_values():
-        other_k[...] = nn(source_row[...], square(5)).astype(LOW)
-        other_v[...] = nn(source_row[...], square(6)).astype(LOW)
+        @pl.loop(0, 2)
+        def _(tile):
+            rows = rows_of(tile, half)
+            other_k[rows] = nn(source_row[rows], square(5)).astype(LOW)
+            other_v[rows] = nn(source_row[rows], square(6)).astype(LOW)
 
     def attend_cross(after):
         flip_heads(other_v, flipped)
@@ -1343,28 +1362,40 @@
             grad_second[part] = normalize_back(grad, normal_mid, inverse_mid, norm_gain[1:2])
 
     def wide_grad(index, left, right):
-        for side in (slice(0, hidden // 2), slice(hidden // 2, hidden)):
-            total = tn(left[...], right[:, side]).astype(LOW)
-            grad_wides[index, :, :, :, side] = total.reshape(4, 2, features // 8, hidden // 2)
+        @pl.loop(0, 2)
+        def _(side):
+            lanes = rows_of(side, hidden // 2)
+            total = tn(left[...], right[:, lanes]).astype(LOW)
+            grad_wides[index, :, :, :, lanes] = total.reshape(4, 2, features // 8, hidden // 2)
 
     def square_grad(index, inputs, grad):
-        grad_squares[index] = tn(inputs, grad).astype(LOW).reshape(grad_squares.shape[1:])
+        @pl.loop(0, 2)
+        def _(side):
+            left = inputs[:, rows_of(side, features // 2)].astype(LOW)
+            total = tn(left, grad[...]).astype(LOW)
+            total = total.reshape(2, 2, features // 8, features)
+            grad_squares[index, pl.ds(2 * side, 2)] = total
 
     def out_back(first, context, inverses, kept):
         for index in range(4):
             Kept(kept, pre, kept_sems).load(index).start()
-        grad = grad_second[...].astype(LOW)
-        square_grad(first + 3, grad, context[...])
+        square_grad(first + 3, grad_second, context)
         lane = lax.broadcasted_iota(jnp.int32, (HEADS, features), 1)
         head = lax.broadcasted_iota(jnp.int32, (HEADS, features), 0)
-        spread = lax.dot_general(
-            inverses[...],
-            jnp.where(lane // 64 == head, 1.0, 0.0),
-            (((0,), (0,)), ((), ())),
-            precision=lax.Precision.HIGHEST,
-            preferred_element_type=WIDE,
-        )
-        cotangent_low[...] = (nn(grad, square(first + 3)) * spread).astype(LOW)
+        pick = jnp.where(lane // 64 == head, 1.0, 0.0)
+
+        @pl.loop(0, 2)
+        def _(tile):
+            rows = rows_of(tile, half)
+            spread = lax.dot_general(
+                inverses[:, rows],
+                pick,
+                (((0,), (0,)), ((), ())),
+                precision=lax.Precision.HIGHEST,
+                preferred_element_type=WIDE,
+            )
+            grad = nn(grad_second[rows].astype(LOW), square(first + 3))
+            cotangent_low[rows] = (grad * spread).astype(LOW)
 
     def attend_back_with(keys, queries, values, context, kept, tile_of, after):
         flip_heads(keys, flipped)
@@ -1377,12 +1408,16 @@
         grad_v[...] = value_sum[...].astype(LOW)
 
     def cross_grads():
-        square_grad(4, hidden_one[...], grad_q[...])
-        square_grad(5, source_row[...], grad_k[...])
-        square_grad(6, source_row[...], grad_v[...])
+        square_grad(4, hidden_one, grad_q)
+        square_grad(5, source_row, grad_k)
+        square_grad(6, source_row, grad_v)
 
     def fill_source_grad():
-        source_row[...] = (nt(grad_k[...], square(5)) + nt(grad_v[...], square(6))).astype(LOW)
+        @pl.loop(0, 2)
+        def _(tile):
+            rows = rows_of(tile, half)
+            grad = nt(grad_k[rows], square(5)) + nt(grad_v[rows], square(6))
+            source_row[rows] = grad.astype(LOW)
 
     def first_norm_back():
         @pl.loop(0, length // 256)
@@ -1436,9 +1471,9 @@
             query_grad=fill_query_grad,
             far_embed_grad=lambda: fill_embed_grad(far_half),
             near_embed_grad=lambda: fill_embed_grad(near_half),
-            key_grad=lambda: square_grad(1, embed_row[...], grad_k[...]),
-            value_grad=lambda: square_grad(2, embed_row[...], grad_v[...]),
-            query_weight_grad=lambda: square_grad(0, query_row[...], grad_q[...]),
+            key_grad=lambda: square_grad(1, embed_row, grad_k),
+            value_grad=lambda: square_grad(2, embed_row, grad_v),
+            query_weight_grad=lambda: square_grad(0, query_row, grad_q),
         ),
     )
 

time: 199 us -> 191 us (0.960); the launches traced: 195 us -> 191 us
  Pallas kernels: 194 us -> 190 us
    pallas_call x1, Pallas kernels: 188 us -> 183 us  [run_layer(): pl.pallas_call(layer_kernel, out_shape=[shape((8, features // 8, features...]
where the time goes in v2:
time: 191 us
  Pallas kernels  190 us (99%)
    pallas_call x1, Pallas kernels, run_layer(): pl.pallas_call(layer_kernel, out_shape=[shape((8, features // 8, features...  183 us
    pallas_call x1, Pallas kernels, write_outputs(): pl.pallas_call(outputs_kernel, grid=(rows,), out_shape=[shape(blocks[0].s...  6.16 us

profile of v2, /device:TPU:0, one launch (start us, length us, event | category | flops | bytes accessed | tf_op | source)
XLA Modules:
  0.0 190.5 jit_solution(311795937113132984)
XLA Ops:
  0.7 183.5 %layer.1 = (f32[8,64,128]{2,1,0:T(8,128)}, f32[2,64,512]{2,1,0:T(8,128)}, f32[8,2048]{1,0:T(8,128)}, bf16[4,256,512]{2,1,0:T(8,128)(2,1)}, bf16[4,256,512]{2,1,0...) custom-call(bf16[4,256,512]{2,1,0:T(8,128)(2,1)} %query.1, ...), custom_call_target="tpu_custom_call" | custom-call | tf_op jit(solution)/shard_map/layer/pallas_call | solution.py:1495
  184.2 6.2 %outputs.1 = (bf16[4,256,512]{2,1,0:T(8,128)(2,1)}, f32[4,256,512]{2,1,0:T(8,128)}, f32[4,256,512]{2,1,0:T(8,128)}, f32[4,256,512]{2,1,0:T(8,128)}, f32[64,128]{...) custom-call(f32[8,64,128]{2,1,0:T(8,128)} %get-tuple-element.43.squa, ...), custom_call_target="tpu_custom_call" | custom-call | tf_op jit(solution)/shard_map/outputs/pallas_call | solution.py:1580
